TPU v7x, 32 devices: a whole 2x2x4 slice. The times are simulated.
32 devices in a mesh: dp: 32 (over z, y, x, core).
Axes of the slice: x: 2, y: 2, z: 4, core: 2. Of those that a mesh axis runs over, the one named last changes fastest.
Arguments:
- image_pooled: bfloat16 [12288, 1152], P('dp'), may hold values from -24 to 24
- text_embed: bfloat16 [12288, 1152], P('dp'), may hold values from -40 to 40
- head_weight: bfloat16 [1152, 1152], replicated, may hold values from -1.4 to 1.4
- logit_scale: float32 [1], replicated, may hold values from 3 to 10
- logit_bias: float32 [1], replicated, may hold values from -2 to 1
Outputs:
- row_loss: float32 [12288], P('dp')
- text_grad: float32 [12288, 1152], P('dp')
- head_grad: float32 [1152, 1152], replicated
All inputs are finite; a program needn't handle non-finite values.
Results may differ from a plain program's by a relative error of at most 0.0003.
Values may be sent and summed in bfloat16 or wider, within the bound.
A program may use at most 128 MiB of HBM per device.

v0:
```python
import jax
import jax.numpy as jnp
from jax import lax
from jax.sharding import PartitionSpec as P

STEPS = 4


epsilon = 1e-06


def shifted(value, axis, steps):
    count = lax.axis_size(axis)
    pairs = [(source, (source + steps) % count) for source in range(count)]
    return lax.ppermute(value, axis, pairs)


def shards(image_pooled, text_embed, head_weight, logit_scale, logit_bias):
    projected = jnp.dot(image_pooled, head_weight, preferred_element_type=jnp.float32)
    inv_img = lax.rsqrt(jnp.sum(projected * projected, axis=1, keepdims=True) + epsilon)
    img_unit = projected * inv_img
    img_bf = img_unit.astype(jnp.bfloat16)
    text_float = text_embed.astype(jnp.float32)
    inv_txt = lax.rsqrt(jnp.sum(text_float * text_float, axis=1, keepdims=True) + epsilon)
    txt_unit = text_float * inv_txt
    txt_bf = txt_unit.astype(jnp.bfloat16)
    local_rows = image_pooled.shape[0]
    identity = jnp.eye(local_rows, dtype=jnp.float32)
    temper = logit_scale[0]
    offset_bias = logit_bias[0]

    def pair_block(images, texts, target):
        scores = lax.dot_general(
            images, texts, (((1,), (1,)), ((), ())), preferred_element_type=jnp.float32
        )
        logits = temper * scores + offset_bias
        loss_part = -jnp.sum(jax.nn.log_sigmoid(target * logits), axis=1)
        coefficient = (-target * temper * jax.nn.sigmoid(-target * logits)).astype(jnp.bfloat16)
        return (loss_part, coefficient)

    def text_side(coefficient, images):
        return lax.dot_general(
            coefficient, images, (((0,), (0,)), ((), ())), preferred_element_type=jnp.float32
        )

    txt_block = txt_bf
    img_block = img_bf
    row_total = jnp.zeros((local_rows,), jnp.float32)
    img_grad = jnp.zeros(img_unit.shape, jnp.float32)
    unit_grad = None
    for offset in range(STEPS):
        if offset > 0:
            txt_block = shifted(txt_block, "dp", 1)
            img_block = shifted(img_block, "dp", -1)
        if offset == 0:
            target = 2.0 * identity - 1.0
        else:
            target = -jnp.ones_like(identity)
        loss_part, coefficient = pair_block(img_bf, txt_block, target)
        row_total = row_total + loss_part
        img_grad = img_grad + jnp.dot(coefficient, txt_block, preferred_element_type=jnp.float32)
        if offset == 0:
            unit_grad = text_side(coefficient, img_bf)
        else:
            mirrored = pair_block(img_block, txt_bf, target)[1]
            unit_grad = unit_grad + text_side(mirrored, img_block)
    row_loss = row_total / (STEPS * local_rows)
    text_grad = (
        unit_grad - txt_unit * jnp.sum(txt_unit * unit_grad, axis=1, keepdims=True)
    ) * inv_txt
    proj_grad = (
        (img_grad - img_unit * jnp.sum(img_unit * img_grad, axis=1, keepdims=True)) * inv_img
    ).astype(jnp.bfloat16)
    partial_head = lax.dot_general(
        image_pooled, proj_grad, (((0,), (0,)), ((), ())), preferred_element_type=jnp.float32
    )
    partial_head = partial_head / lax.axis_size("dp")
    head_grad = lax.psum(partial_head, "dp")
    return (row_loss, text_grad, head_grad)


def solution(mesh):
    in_specs = (P("dp", None), P("dp", None), P(), P(), P())
    out_specs = (P("dp"), P("dp", None), P())
    return jax.shard_map(shards, mesh=mesh, in_specs=in_specs, out_specs=out_specs, check_vma=False)
```

profile of v0, /device:TPU:0, one launch (start us, length us, event | category | flops | bytes accessed | tf_op | source)
XLA Modules:
  0.0 238.8 jit_solution(6039109724754947120)
XLA Ops:
  7.2 0.0 all-reduce.2.cloned.1.call-start
  7.2 1.6 fusion.7
  8.8 1.4 fusion.3
  10.2 0.5 collective-permute-start
  10.7 1.6 multiply_reduce_fusion.1
  12.3 0.2 multiply_convert_fusion.1
  12.5 6.0 %collective-permute-start.3 = (bf16[384,1152]{1,0:T(8,128)(2,1)S(1)}, bf16[384,1152]{1,0:T(8,128)(2,1)}, u32[]{:S(2)}, u32[]{:S(2)}) collective-permute-start(bf16[384,1152]{1,0:T(8,128)(2,1)S(1)} %multiply_convert_fusion.1), channel_id=1, source_target_pairs={{0,31},{1,0},{2,1},{3,2},{4,3},{5,4},{6,5},{7,6},{8,7},{9,8},{10,9... | collective-permute-start | bytes 2654216 | tf_op jit(solution)/shard_map/ppermute | solution.py:15
  18.5 9.0 %collective-permute-done = bf16[384,1152]{1,0:T(8,128)(2,1)S(1)} collective-permute-done((bf16[384,1152]{1,0:T(8,128)(2,1)S(1)}, bf16[384,1152]{1,0:T(8,128)(2,1)S(1)}, u32[]{:S(2)}, u32[]{:S(2)}) %collective-permute-start) | collective-permute-done | bytes 884768 | tf_op jit(solution)/shard_map/ppermute | solution.py:15
  27.5 5.3 %collective-permute-start.1 = (bf16[384,1152]{1,0:T(8,128)(2,1)S(1)}, bf16[384,1152]{1,0:T(8,128)(2,1)S(1)}, u32[]{:S(2)}, u32[]{:S(2)}) collective-permute-start(bf16[384,1152]{1,0:T(8,128)(2,1)S(1)} %collective-permute-done), channel_id=1, source_target_pairs={{0,1},{1,2},{2,3},{3,4},{4,5},{5,6},{6,7},{7,8},{8,9},{9,10},{10,1... | collective-permute-start | bytes 2654216 | tf_op jit(solution)/shard_map/ppermute | solution.py:15
  34.1 1.0 fusion.35
  35.1 0.8 fusion.60
  36.0 0.1 collective-permute-start.4
  36.1 1.0 fusion.36
  37.1 6.6 %collective-permute-done.1 = bf16[384,1152]{1,0:T(8,128)(2,1)S(1)} collective-permute-done((bf16[384,1152]{1,0:T(8,128)(2,1)S(1)}, bf16[384,1152]{1,0:T(8,128)(2,1)S(1)}, u32[]{:S(2)}, u32[]{:S(2)}) %collective-permute-start.1) | collective-permute-done | bytes 884768 | tf_op jit(solution)/shard_map/ppermute | solution.py:15
  43.6 11.1 %collective-permute-start.2 = (bf16[384,1152]{1,0:T(8,128)(2,1)S(1)}, bf16[384,1152]{1,0:T(8,128)(2,1)S(1)}, u32[]{:S(2)}, u32[]{:S(2)}) collective-permute-start(bf16[384,1152]{1,0:T(8,128)(2,1)S(1)} %collective-permute-done.1), channel_id=1, source_target_pairs={{0,1},{1,2},{2,3},{3,4},{4,5},{5,6},{6,7},{7,8},{8,9},{9,10},{10,1... | collective-permute-start | bytes 2654216 | tf_op jit(solution)/shard_map/ppermute | solution.py:15
  54.7 0.7 convolution_add_fusion.2
  55.4 1.0 fusion.37
  56.4 0.7 convolution_add_fusion.1
  57.1 2.7 %collective-permute-done.2 = bf16[384,1152]{1,0:T(8,128)(2,1)S(1)} collective-permute-done((bf16[384,1152]{1,0:T(8,128)(2,1)S(1)}, bf16[384,1152]{1,0:T(8,128)(2,1)S(1)}, u32[]{:S(2)}, u32[]{:S(2)}) %collective-permute-start.2) | collective-permute-done | bytes 884768 | tf_op jit(solution)/shard_map/ppermute | solution.py:15
  59.8 1.6 fusion.38
  61.4 1.0 multiply_reduce_fusion
  62.4 0.2 copy-done.4
  62.5 4.3 %fusion = f32[1152,1152]{0,1:T(8,128)} fusion(bf16[384,1152]{1,0:T(8,128)(2,1)S(1)} %copy-done.4, f32[384,1152]{1,0:T(8,128)S(1)} %get-tuple-element.19, f32[384,1152]{1,0:T(8,128)S(1)} %get-tuple-element.7, f32[384]{0:T(512)S(1)} %get-tuple-element.18, f32[384]{0:T(512)S(1)} %add_rsqrt_fusion.1), kind=kOutput, calls=%fused_computation.1 | convolution fusion | flops 1022754816 | bytes 9735168 | tf_op jit(solution)/shard_map/dot_general | solution.py:74
  66.8 3.2 %fusion.61 = f32[384,1152]{1,0:T(8,128)} fusion(bf16[384,1152]{1,0:T(8,128)(2,1)} %copy-done.2, f32[384,384]{0,1:T(8,128)} %copy-done.5, f32[]{:T(128)} %bitcast.31), kind=kOutput, calls=%fused_computation.94 | convolution fusion | flops 341360640 | bytes 3244036 | tf_op jit(solution)/shard_map/dot_general | solution.py:42
  70.1 4.6 %convolution_add_fusion.5 = f32[384,1152]{1,0:T(8,128)} fusion(f32[384,1152]{1,0:T(8,128)} %fusion.61, bf16[384,1152]{1,0:T(8,128)(2,1)} %collective-permute-done.3, f32[]{:T(128)} %bitcast.39, f32[]{:T(128)} %bitcast.29, bf16[384,1152]{1,0:T(8,128)(2,1)S(1)} %copy-done.1, f32[384]{0:T(512)S(1)} %add_rsqrt_fusion), kind=kOutput, calls=%fused_computation.7 | convolution fusion | flops 682278912 | bytes 5309960 | tf_op jit(solution)/shard_map/dot_general | solution.py:42
  74.6 4.6 %convolution_add_fusion.4 = f32[384,1152]{1,0:T(8,128)} fusion(f32[384,1152]{1,0:T(8,128)} %convolution_add_fusion.5, bf16[384,1152]{1,0:T(8,128)(2,1)} %collective-permute-done.4, f32[]{:T(128)} %bitcast.38, f32[]{:T(128)} %bitcast.27, bf16[384,1152]{1,0:T(8,128)(2,1)S(1)} %copy-done.1, f32[384]{0:T(512)S(1)} %add_rsqrt_fusion), kind=kOutput, calls=%fused_computation.6 | convolution fusion | flops 682278912 | bytes 5309960 | tf_op jit(solution)/shard_map/dot_general | solution.py:42
  79.2 1.3 add_multiply_fusion
  80.5 0.4 collective-permute-done.5
  80.9 4.8 %fusion.4 = (f32[384]{0:T(512)S(1)}, f32[384,1152]{1,0:T(8,128)}) fusion(bf16[384,1152]{1,0:T(8,128)(2,1)S(1)} %copy-done.1, f32[384]{0:T(512)S(1)} %add_rsqrt_fusion, f32[384,1152]{1,0:T(8,128)} %convolution_add_fusion.4, bf16[384,1152]{1,0:T(8,128)(2,1)} %collective-permute-done.5, f32[]{:T(128)} %bitcast.37, f32[]{:T(128)} %bitcast.25), kind=kOutput, calls=%fused_computation.13 | convolution fusion | flops 684048000 | bytes 5311496 | tf_op jit(solution)/shard_map/dot_general | solution.py:42
  85.7 3.1 %fusion.6 = f32[384,1152]{1,0:T(8,128)} fusion(f32[384,1152]{1,0:T(8,128)} %get-tuple-element.17, bf16[384,1152]{1,0:T(8,128)(2,1)S(1)} %copy-done.1, f32[384]{0:T(512)S(1)} %get-tuple-element.16, f32[384]{0:T(512)S(1)} %add_rsqrt_fusion), kind=kLoop, calls=%fused_computation.15 | loop fusion | flops 2211840 | bytes 4426752 | tf_op jit(solution)/shard_map/mul | solution.py:68
  88.8 136.2 %all-reduce.2.cloned.1.call-done = f32[1152,1152]{0,1:T(8,128)} async-done(((f32[1152,1152]{0,1:T(8,128)}), f32[1152,1152]{0,1:T(8,128)}) %all-reduce.2.cloned.1.call-update) | async-done | bytes 5308432 | tf_op jit(solution)/shard_map/psum | solution.py:78
  225.1 6.9 %copy.8 = f32[1152,1152]{1,0:T(8,128)} copy(f32[1152,1152]{0,1:T(8,128)} %all-reduce.2.cloned.1.call-done) | data formatting | bytes 10616832
  (17 shorter events, 0.1 us)
Async XLA Ops:
  7.2 3.5 %copy-start = (bf16[1152,1152]{1,0:T(8,128)(2,1)S(1)}, bf16[1152,1152]{1,0:T(8,128)(2,1)}, u32[]{:S(2)}) copy-start(bf16[1152,1152]{1,0:T(8,128)(2,1)} %param.7) | copy-start | bytes 7962628
  7.2 3.5 %copy-start.3 = (bf16[384,1152]{1,0:T(8,128)(2,1)S(1)}, bf16[384,1152]{1,0:T(8,128)(2,1)}, u32[]{:S(2)}) copy-start(bf16[384,1152]{1,0:T(8,128)(2,1)} %param.5) | copy-start | bytes 2654212
  7.2 217.9 %all-reduce.2.cloned.1.call-start = ((), (), s32[]{:S(2)}) async-start(), calls=%async_computation | async-start | bytes 10616832 | tf_op jit(solution)/shard_map/psum | solution.py:78
  10.2 17.3 %collective-permute-start = (bf16[384,1152]{1,0:T(8,128)(2,1)S(1)}, bf16[384,1152]{1,0:T(8,128)(2,1)S(1)}, u32[]{:S(2)}, u32[]{:S(2)}) collective-permute-start(bf16[384,1152]{1,0:T(8,128)(2,1)S(1)} %fusion.3), channel_id=1, source_target_pairs={{0,1},{1,2},{2,3},{3,4},{4,5},{5,6},{6,7},{7,8},{8,9},{9,10},{10,1... | collective-permute-start | bytes 2654216 | tf_op jit(solution)/shard_map/ppermute | solution.py:15
  12.3 21.8 %copy-start.1 = (bf16[384,1152]{1,0:T(8,128)(2,1)S(1)}, bf16[384,1152]{1,0:T(8,128)(2,1)}, u32[]{:S(2)}) copy-start(bf16[384,1152]{1,0:T(8,128)(2,1)} %param.6) | copy-start | bytes 2654212
  12.5 47.3 %copy-start.2 = (bf16[384,1152]{1,0:T(8,128)(2,1)}, bf16[384,1152]{1,0:T(8,128)(2,1)S(1)}, u32[]{:S(2)}) copy-start(bf16[384,1152]{1,0:T(8,128)(2,1)S(1)} %multiply_convert_fusion.1) | copy-start | bytes 2654212
  12.5 23.5 %collective-permute-start.3 = (bf16[384,1152]{1,0:T(8,128)(2,1)S(1)}, bf16[384,1152]{1,0:T(8,128)(2,1)}, u32[]{:S(2)}, u32[]{:S(2)}) collective-permute-start(bf16[384,1152]{1,0:T(8,128)(2,1)S(1)} %multiply_convert_fusion.1), channel_id=1, source_target_pairs={{0,31},{1,0},{2,1},{3,2},{4,3},{5,4},{6,5},{7,6},{8,7},{9,8},{10,9... | collective-permute-start | bytes 2654216 | tf_op jit(solution)/shard_map/ppermute | solution.py:15
  27.5 16.2 %collective-permute-start.1 = (bf16[384,1152]{1,0:T(8,128)(2,1)S(1)}, bf16[384,1152]{1,0:T(8,128)(2,1)S(1)}, u32[]{:S(2)}, u32[]{:S(2)}) collective-permute-start(bf16[384,1152]{1,0:T(8,128)(2,1)S(1)} %collective-permute-done), channel_id=1, source_target_pairs={{0,1},{1,2},{2,3},{3,4},{4,5},{5,6},{6,7},{7,8},{8,9},{9,10},{10,1... | collective-permute-start | bytes 2654216 | tf_op jit(solution)/shard_map/ppermute | solution.py:15
  35.1 0.9 copy-start.5
  36.0 34.0 %collective-permute-start.4 = (bf16[384,1152]{1,0:T(8,128)(2,1)}, bf16[384,1152]{1,0:T(8,128)(2,1)}, u32[]{:S(2)}, u32[]{:S(2)}) collective-permute-start(bf16[384,1152]{1,0:T(8,128)(2,1)} %collective-permute-done.3), channel_id=1, source_target_pairs={{0,31},{1,0},{2,1},{3,2},{4,3},{5,4},{6,5},{7,6},{8,7},{9,8},{10,9... | collective-permute-start | bytes 2654216 | tf_op jit(solution)/shard_map/ppermute | solution.py:15
  43.6 16.2 %collective-permute-start.2 = (bf16[384,1152]{1,0:T(8,128)(2,1)S(1)}, bf16[384,1152]{1,0:T(8,128)(2,1)S(1)}, u32[]{:S(2)}, u32[]{:S(2)}) collective-permute-start(bf16[384,1152]{1,0:T(8,128)(2,1)S(1)} %collective-permute-done.1), channel_id=1, source_target_pairs={{0,1},{1,2},{2,3},{3,4},{4,5},{5,6},{6,7},{7,8},{8,9},{9,10},{10,1... | collective-permute-start | bytes 2654216 | tf_op jit(solution)/shard_map/ppermute | solution.py:15
  61.4 1.2 copy-start.4
  70.1 10.9 %collective-permute-start.5 = (bf16[384,1152]{1,0:T(8,128)(2,1)}, bf16[384,1152]{1,0:T(8,128)(2,1)}, u32[]{:S(2)}, u32[]{:S(2)}) collective-permute-start(bf16[384,1152]{1,0:T(8,128)(2,1)} %collective-permute-done.4), channel_id=1, source_target_pairs={{0,31},{1,0},{2,1},{3,2},{4,3},{5,4},{6,5},{7,6},{8,7},{9,8},{10,9... | collective-permute-start | bytes 2654216 | tf_op jit(solution)/shard_map/ppermute | solution.py:15
Sparse Core Ops, SparseCore 0:
  66.9 158.0 all-reduce.1
where the time goes:
time: 239 us
  waiting for transfers between devices  155 us (65%)
  matrix products  30.8 us (13%)
  starting transfers between devices  23.1 us (10%)
  between operations  15.4 us (6%)
  other arithmetic  7.47 us (3%)
  local copies, waits for them, and re-layouts  7.05 us (3%)
    psum x1, waiting for transfers between devices, shards(): head_grad = lax.psum(partial_head, 'dp')  136 us
    ppermute x6, starting transfers between devices, shifted(): return lax.ppermute(value, axis, pairs)  23 us
    ppermute x6, waiting for transfers between devices, shifted(): return lax.ppermute(value, axis, pairs)  18.7 us
    dot_general x4, matrix products, text_side(): lax.dot_general(coefficient, images, (((0,), (0,)), ((), ())), preferred_...  17.2 us
    unnamed x13, local copies, waits for them, and re-layouts  7.05 us
  transfers between devices with their start and end apart: 7, of which 5 were waited for; matrix products, arithmetic and copies ran while one was open for 15% of the time, Pallas kernels for 0%

commit v1 on v0

--- a/solution.py
+++ b/solution.py
@@ -1,9 +1,16 @@
+import functools
+
 import jax
 import jax.numpy as jnp
 from jax import lax
+from jax.experimental import pallas as pl
+from jax.experimental.pallas import tpu as pltpu
 from jax.sharding import PartitionSpec as P
 
 STEPS = 4
+PARTS = 3
+TILE = 8
+LANES = 128
 
 
 epsilon = 1e-06
@@ -13,6 +20,158 @@
     count = lax.axis_size(axis)
     pairs = [(source, (source + steps) % count) for source in range(count)]
     return lax.ppermute(value, axis, pairs)
+
+
+def bit_orders(count):
+    levels = count.bit_length() - 1
+    middle = list(range(1, levels - 1))
+    orders = []
+    for part in range(PARTS):
+        turn = part % max(len(middle), 1)
+        orders.append([0] + middle[turn:] + middle[:turn] + [levels - 1])
+    return orders
+
+
+def bit_of(me, bit):
+    return lax.rem(lax.div(me, 1 << bit), 2)
+
+
+def partner_of(me, bit):
+    return me + (1 - 2 * bit_of(me, bit)) * (1 << bit)
+
+
+def greet(me, levels):
+    barrier = pltpu.get_barrier_semaphore()
+    for bit in range(levels):
+        pl.semaphore_signal(
+            barrier, inc=1, device_id=(partner_of(me, bit),), device_id_type=pl.DeviceIdType.MESH
+        )
+    pl.semaphore_wait(barrier, levels)
+
+
+def sum_kernel(count, chunk, a_ref, g_ref, out_ref, total, landed, send_sem, recv_sem, back_send, back_recv):
+    me = lax.axis_index("dp")
+    orders = bit_orders(count)
+    levels = count.bit_length() - 1
+    width = a_ref.shape[1] // PARTS
+    blocks = g_ref.shape[1] // LANES
+    rows = width // TILE
+    used = blocks * rows
+    full = count * chunk
+    greet(me, levels)
+
+    def copy_at(part, step, start):
+        half = full >> (step + 1)
+        bit = orders[part][step]
+        base = full - (full >> step)
+        return pltpu.make_async_remote_copy(
+            src_ref=total.at[part, pl.ds(start + (1 - bit_of(me, bit)) * half, half)],
+            dst_ref=landed.at[part, pl.ds(base, half)],
+            send_sem=send_sem.at[part, step],
+            recv_sem=recv_sem.at[part, step],
+            device_id=(partner_of(me, bit),),
+            device_id_type=pl.DeviceIdType.MESH,
+        )
+
+    def add(part, where, source, length):
+        size = chunk
+        while size < 8 and length % (2 * size) == 0:
+            size *= 2
+
+        def body(i, carry):
+            total[part, pl.ds(where + i * size, size)] += landed[part, pl.ds(source + i * size, size)]
+            return carry
+
+        lax.fori_loop(0, length // size, body, 0)
+
+    copies = {}
+    starts = [0] * PARTS
+    for part in range(PARTS):
+        product = lax.dot_general(
+            a_ref[:, part * width:(part + 1) * width], g_ref[...],
+            (((0,), (0,)), ((), ())), preferred_element_type=jnp.float32,
+        )
+        for block in range(blocks):
+            total[part, pl.ds(block, rows, stride=blocks)] = product[
+                :, block * LANES:(block + 1) * LANES
+            ].reshape(rows, TILE, LANES)
+        if full > used:
+            total[part, used:] = jnp.zeros((full - used, TILE, LANES), jnp.float32)
+        copies[part, 0] = copy_at(part, 0, 0)
+        copies[part, 0].start()
+    for step in range(levels):
+        half = full >> (step + 1)
+        base = full - (full >> step)
+        for part in range(PARTS):
+            copies[part, step].wait_recv()
+            start = starts[part] + bit_of(me, orders[part][step]) * half
+            starts[part] = start
+            if step + 1 < levels:
+                quarter = half // 2
+                mine = bit_of(me, orders[part][step + 1])
+                away, kept = (1 - mine) * quarter, mine * quarter
+                add(part, start + away, base + away, quarter)
+                copies[part, step + 1] = copy_at(part, step + 1, start)
+                copies[part, step + 1].start()
+                add(part, start + kept, base + kept, quarter)
+            else:
+                out_ref[part, pl.ds(start, half)] = (
+                    total[part, pl.ds(start, half)] + landed[part, pl.ds(base, half)]
+                ) * (1.0 / count)
+    backs = {}
+    for step in reversed(range(levels)):
+        length = full >> (step + 1)
+        for part in range(PARTS):
+            if step + 1 < levels:
+                backs[part, step + 1].wait_recv()
+                bit = orders[part][step + 1]
+                starts[part] = starts[part] - bit_of(me, bit) * (length // 2)
+            where = out_ref.at[part, pl.ds(starts[part], length)]
+            backs[part, step] = pltpu.make_async_remote_copy(
+                src_ref=where,
+                dst_ref=where,
+                send_sem=back_send.at[part, step],
+                recv_sem=back_recv.at[part, step],
+                device_id=(partner_of(me, orders[part][step]),),
+                device_id_type=pl.DeviceIdType.MESH,
+            )
+            backs[part, step].start()
+    for part in range(PARTS):
+        backs[part, 0].wait_recv()
+    for copy in copies.values():
+        copy.wait_send()
+    for copy in backs.values():
+        copy.wait_send()
+
+
+def summed_head(image_pooled, proj_grad):
+    count = lax.axis_size("dp")
+    levels = count.bit_length() - 1
+    depth, width = image_pooled.shape[1], proj_grad.shape[1]
+    used = depth * width // (PARTS * TILE * LANES)
+    chunk = -(-used // count)
+    full = chunk * count
+    vmem = pl.BlockSpec(memory_space=pltpu.VMEM)
+    every = pl.pallas_call(
+        functools.partial(sum_kernel, count, chunk),
+        out_shape=jax.ShapeDtypeStruct((PARTS, full, TILE, LANES), jnp.float32),
+        in_specs=[vmem, vmem],
+        out_specs=vmem,
+        scratch_shapes=[
+            pltpu.VMEM((PARTS, full, TILE, LANES), jnp.float32),
+            pltpu.VMEM((PARTS, full, TILE, LANES), jnp.float32),
+            pltpu.SemaphoreType.DMA((PARTS, levels)),
+            pltpu.SemaphoreType.DMA((PARTS, levels)),
+            pltpu.SemaphoreType.DMA((PARTS, levels)),
+            pltpu.SemaphoreType.DMA((PARTS, levels)),
+        ],
+        compiler_params=pltpu.CompilerParams(
+            collective_id=0, has_side_effects=True, vmem_limit_bytes=40 * 1024 * 1024
+        ),
+        name="head_sum",
+    )(image_pooled, proj_grad)
+    values = every[:, :used].reshape(depth // TILE, width // LANES, TILE, LANES)
+    return values.transpose(0, 2, 1, 3).reshape(depth, width)
 
 
 def shards(image_pooled, text_embed, head_weight, logit_scale, logit_bias):
@@ -71,11 +230,7 @@
     proj_grad = (
         (img_grad - img_unit * jnp.sum(img_unit * img_grad, axis=1, keepdims=True)) * inv_img
     ).astype(jnp.bfloat16)
-    partial_head = lax.dot_general(
-        image_pooled, proj_grad, (((0,), (0,)), ((), ())), preferred_element_type=jnp.float32
-    )
-    partial_head = partial_head / lax.axis_size("dp")
-    head_grad = lax.psum(partial_head, "dp")
+    head_grad = summed_head(image_pooled, proj_grad)
     return (row_loss, text_grad, head_grad)
 
 

time: 239 us -> 159 us (0.67)
  waiting for transfers between devices: 155 us -> 4.04 us
  Pallas kernels: 0 us -> 79 us
  between operations: 15.4 us -> 2.06 us
  matrix products: 30.8 us -> 36.4 us
  local copies, waits for them, and re-layouts: 7.05 us -> 2.77 us
  starting transfers between devices: 23.1 us -> 26.8 us
    psum x1 -> x0, waiting for transfers between devices: 136 us -> none  [shards(): head_grad = lax.psum(partial_head, 'dp')]
    pallas_call x0 -> x1, Pallas kernels: none -> 79 us  [summed_head(): pl.pallas_call(functools.partial(sum_kernel, count, chunk), out_shape=jax...]
    ppermute x6, waiting for transfers between devices: 18.7 us -> 4.04 us  [shifted(): return lax.ppermute(value, axis, pairs)]
    unnamed x13 -> x22, local copies, waits for them, and re-layouts: 7.05 us -> 0.05 us
    dot_general x4, matrix products: 3.27 us -> 9.29 us  [shards(): jnp.dot(coefficient, txt_block, preferred_element_type=jnp.float32)]
    dot_general x4, matrix products: 4.54 us -> 9.43 us  [pair_block(): lax.dot_general(images, texts, (((1,), (1,)), ((), ())), preferred_elemen...]
    dot_general x1 -> x0, matrix products: 4.27 us -> none  [shards(): lax.dot_general(image_pooled, proj_grad, (((0,), (0,)), ((), ())), prefer...]
    ppermute x6, starting transfers between devices: 23 us -> 26.8 us  [shifted(): return lax.ppermute(value, axis, pairs)]
  transfers between devices with their start and end apart: 7 -> 6, of which waited for: 5 -> 1; matrix products, arithmetic and copies ran while one was open for 15% -> 22% of each run, Pallas kernels for 0% -> 50%
where the time goes in v1:
time: 159 us; the launch traced here: 158 us
  Pallas kernels  79 us (50%)
  matrix products  36.4 us (23%)
  starting transfers between devices  26.8 us (17%)
  other arithmetic  7.1 us (4%)
  waiting for transfers between devices  4.04 us (3%)
  local copies, waits for them, and re-layouts  2.77 us (2%)
  between operations  2.06 us (1%)
    pallas_call x1, Pallas kernels, summed_head(): pl.pallas_call(functools.partial(sum_kernel, count, chunk), out_shape=jax...  79 us
    ppermute x6, starting transfers between devices, shifted(): return lax.ppermute(value, axis, pairs)  26.8 us
    dot_general x4, matrix products, text_side(): lax.dot_general(coefficient, images, (((0,), (0,)), ((), ())), preferred_...  16.2 us
    dot_general x4, matrix products, pair_block(): lax.dot_general(images, texts, (((1,), (1,)), ((), ())), preferred_elemen...  9.43 us
    dot_general x4, matrix products, shards(): jnp.dot(coefficient, txt_block, preferred_element_type=jnp.float32)  9.29 us
    ppermute x6, waiting for transfers between devices, shifted(): return lax.ppermute(value, axis, pairs)  4.04 us
  transfers between devices with their start and end apart: 6, of which 1 were waited for; matrix products, arithmetic and copies ran while one was open for 22% of the time, Pallas kernels for 50%

profile of v1, /device:TPU:0, one launch (start us, length us, event | category | flops | bytes accessed | tf_op | source)
XLA Modules:
  0.0 158.2 jit_solution(7104422594242581555)
XLA Ops:
  0.6 0.0 copy-start
  0.7 1.6 fusion.6
  2.2 1.4 fusion.2
  3.6 0.5 collective-permute-start
  4.1 1.5 multiply_reduce_fusion.1
  5.7 0.0 copy-start.4
  5.7 0.2 multiply_convert_fusion.1
  5.9 6.0 %collective-permute-start.3 = (bf16[384,1152]{1,0:T(8,128)(2,1)S(1)}, bf16[384,1152]{1,0:T(8,128)(2,1)}, u32[]{:S(2)}, u32[]{:S(2)}) collective-permute-start(bf16[384,1152]{1,0:T(8,128)(2,1)S(1)} %multiply_convert_fusion.1), channel_id=1, source_target_pairs={{0,31},{1,0},{2,1},{3,2},{4,3},{5,4},{6,5},{7,6},{8,7},{9,8},{10,9... | collective-permute-start | bytes 2654216 | tf_op jit(solution)/shard_map/ppermute | solution.py:22
  13.2 1.0 fusion.32
  14.2 1.9 %fusion.58 = f32[384,1152]{1,0:T(8,128)} fusion(bf16[384,1152]{1,0:T(8,128)(2,1)S(1)} %multiply_convert_fusion.1, f32[384,384]{0,1:T(8,128)S(1)} %get-tuple-element.10, f32[]{:T(128)} %bitcast.33), kind=kOutput, calls=%fused_computation.90 | convolution fusion | flops 341360640 | bytes 3244036 | tf_op jit(solution)/shard_map/dot_general | solution.py:201
  16.1 0.8 fusion.57
  17.0 4.0 %collective-permute-done = bf16[384,1152]{1,0:T(8,128)(2,1)} collective-permute-done((bf16[384,1152]{1,0:T(8,128)(2,1)S(1)}, bf16[384,1152]{1,0:T(8,128)(2,1)}, u32[]{:S(2)}, u32[]{:S(2)}) %collective-permute-start) | collective-permute-done | bytes 884768 | tf_op jit(solution)/shard_map/ppermute | solution.py:22
  21.0 5.2 %collective-permute-start.1 = (bf16[384,1152]{1,0:T(8,128)(2,1)}, bf16[384,1152]{1,0:T(8,128)(2,1)}, u32[]{:S(2)}, u32[]{:S(2)}) collective-permute-start(bf16[384,1152]{1,0:T(8,128)(2,1)} %collective-permute-done), channel_id=1, source_target_pairs={{0,1},{1,2},{2,3},{3,4},{4,5},{5,6},{6,7},{7,8},{8,9},{9,10},{10,1... | collective-permute-start | bytes 2654216 | tf_op jit(solution)/shard_map/ppermute | solution.py:22
  26.2 2.0 %collective-permute-start.4 = (bf16[384,1152]{1,0:T(8,128)(2,1)}, bf16[384,1152]{1,0:T(8,128)(2,1)}, u32[]{:S(2)}, u32[]{:S(2)}) collective-permute-start(bf16[384,1152]{1,0:T(8,128)(2,1)} %collective-permute-done.3), channel_id=1, source_target_pairs={{0,31},{1,0},{2,1},{3,2},{4,3},{5,4},{6,5},{7,6},{8,7},{9,8},{10,9... | collective-permute-start | bytes 2654216 | tf_op jit(solution)/shard_map/ppermute | solution.py:22
  28.2 2.1 %fusion.33 = (f32[384]{0:T(512)S(1)}, f32[384,384]{0,1:T(8,128)S(1)}) fusion(f32[]{:T(128)} %bitcast.44, bf16[384,1152]{1,0:T(8,128)(2,1)S(1)} %multiply_convert_fusion.1, bf16[384,1152]{1,0:T(8,128)(2,1)} %collective-permute-done, f32[]{:T(128)} %bitcast.36), kind=kOutput, calls=%fused_computation.56 | convolution fusion | flops 341360256 | bytes 2360840 | tf_op jit(solution)/shard_map/dot_general | solution.py:192
  30.3 3.1 %convolution_add_fusion.2 = f32[384,1152]{1,0:T(8,128)} fusion(f32[384,1152]{1,0:T(8,128)S(1)} %fusion.57, bf16[384,1152]{1,0:T(8,128)(2,1)} %collective-permute-done, f32[384,384]{0,1:T(8,128)S(1)} %get-tuple-element.12, f32[]{:T(128)} %bitcast.28), kind=kOutput, calls=%fused_computation.2 | convolution fusion | flops 340918272 | bytes 5013508 | tf_op jit(solution)/shard_map/dot_general | solution.py:220
  33.4 4.9 %convolution_add_fusion.5 = f32[384,1152]{1,0:T(8,128)} fusion(f32[384,1152]{1,0:T(8,128)} %fusion.58, bf16[384,1152]{1,0:T(8,128)(2,1)} %collective-permute-done.3, f32[]{:T(128)} %bitcast.41, f32[]{:T(128)} %bitcast.31, bf16[384,1152]{1,0:T(8,128)(2,1)} %param.6, f32[384]{0:T(512)S(1)} %add_rsqrt_fusion), kind=kOutput, calls=%fused_computation.5 | convolution fusion | flops 682278912 | bytes 5309960 | tf_op jit(solution)/shard_map/dot_general | solution.py:201
  38.3 0.0 collective-permute-done.1
  38.3 9.4 %collective-permute-start.2 = (bf16[384,1152]{1,0:T(8,128)(2,1)}, bf16[384,1152]{1,0:T(8,128)(2,1)}, u32[]{:S(2)}, u32[]{:S(2)}) collective-permute-start(bf16[384,1152]{1,0:T(8,128)(2,1)} %collective-permute-done.1), channel_id=1, source_target_pairs={{0,1},{1,2},{2,3},{3,4},{4,5},{5,6},{6,7},{7,8},{8,9},{9,10},{10,1... | collective-permute-start | bytes 2654216 | tf_op jit(solution)/shard_map/ppermute | solution.py:22
  47.7 3.7 %collective-permute-start.5 = (bf16[384,1152]{1,0:T(8,128)(2,1)}, bf16[384,1152]{1,0:T(8,128)(2,1)}, u32[]{:S(2)}, u32[]{:S(2)}) collective-permute-start(bf16[384,1152]{1,0:T(8,128)(2,1)} %collective-permute-done.4), channel_id=1, source_target_pairs={{0,31},{1,0},{2,1},{3,2},{4,3},{5,4},{6,5},{7,6},{8,7},{9,8},{10,9... | collective-permute-start | bytes 2654216 | tf_op jit(solution)/shard_map/ppermute | solution.py:22
  51.4 3.1 %fusion.34 = (f32[384]{0:T(512)}, f32[384,384]{0,1:T(8,128)S(1)}) fusion(f32[]{:T(128)} %bitcast.43, bf16[384,1152]{1,0:T(8,128)(2,1)} %copy-done.8, bf16[384,1152]{1,0:T(8,128)(2,1)} %collective-permute-done.1, f32[]{:T(128)} %bitcast.35), kind=kOutput, calls=%fused_computation.57 | convolution fusion | flops 341360256 | bytes 2360840 | tf_op jit(solution)/shard_map/dot_general | solution.py:192
  54.5 3.1 %convolution_add_fusion.1 = f32[384,1152]{1,0:T(8,128)} fusion(f32[384,1152]{1,0:T(8,128)S(1)} %copy-done.7, bf16[384,1152]{1,0:T(8,128)(2,1)} %collective-permute-done.1, f32[384,384]{0,1:T(8,128)S(1)} %get-tuple-element.8, f32[]{:T(128)} %bitcast.30), kind=kOutput, calls=%fused_computation.1 | convolution fusion | flops 340918272 | bytes 5013508 | tf_op jit(solution)/shard_map/dot_general | solution.py:220
  57.6 4.9 %convolution_add_fusion.4 = f32[384,1152]{1,0:T(8,128)} fusion(f32[384,1152]{1,0:T(8,128)} %convolution_add_fusion.5, bf16[384,1152]{1,0:T(8,128)(2,1)} %collective-permute-done.4, f32[]{:T(128)} %bitcast.40, f32[]{:T(128)} %bitcast.29, bf16[384,1152]{1,0:T(8,128)(2,1)} %param.6, f32[384]{0:T(512)S(1)} %add_rsqrt_fusion), kind=kOutput, calls=%fused_computation.4 | convolution fusion | flops 682278912 | bytes 5309960 | tf_op jit(solution)/shard_map/dot_general | solution.py:201
  62.5 3.1 %fusion.35 = (f32[384]{0:T(512)}, f32[384,384]{0,1:T(8,128)S(1)}) fusion(f32[]{:T(128)} %bitcast.42, bf16[384,1152]{1,0:T(8,128)(2,1)} %copy-done.8, bf16[384,1152]{1,0:T(8,128)(2,1)} %collective-permute-done.2, f32[]{:T(128)} %bitcast.34), kind=kOutput, calls=%fused_computation.58 | convolution fusion | flops 341360256 | bytes 2360840 | tf_op jit(solution)/shard_map/dot_general | solution.py:192
  65.6 2.2 %multiply_reduce_fusion = (f32[384]{0:T(512)S(1)}, f32[384,1152]{1,0:T(8,128)S(1)}) fusion(f32[384,1152]{1,0:T(8,128)S(1)} %copy-done.3, f32[384]{0:T(512)S(1)} %add_rsqrt_fusion.1, f32[384,1152]{1,0:T(8,128)S(1)} %copy-done.6, bf16[384,1152]{1,0:T(8,128)(2,1)} %collective-permute-done.2, f32[384,384]{0,1:T(8,128)S(1)} %get-tuple-element.6, f32[]{:T(128)} %bitcast.32), kind=kOutput, calls=%fused_computation.16 | convolution fusion | flops 342244992 | bytes 6786052 | tf_op jit(solution)/shard_map/dot_general | solution.py:220
  67.9 0.3 multiply_convert_fusion.g_ref
  68.2 79.0 %head_sum.1 = f32[3,448,8,128]{3,2,1,0:T(8,128)S(1)} custom-call(bf16[384,1152]{1,0:T(8,128)(2,1)S(1)} %copy-done.1, bf16[384,1152]{1,0:T(8,128)(2,1)S(1)} %multiply_convert_fusion.g_ref), custom_call_target="tpu_custom_call" | custom-call | tf_op jit(solution)/shard_map/head_sum/pallas_call | solution.py:155
  147.2 0.0 copy-start.5
  147.2 2.7 %slice.3 = f32[3,432,8,128]{3,2,1,0:T(8,128)} slice(f32[3,448,8,128]{3,2,1,0:T(8,128)S(1)} %head_sum.1), slice={[0:3], [0:432], [0:8], [0:128]} | slice | bytes 10616832 | tf_op jit(solution)/shard_map/slice | solution.py:173
  150.0 4.6 %fusion.3 = (f32[384]{0:T(512)S(1)}, f32[384,1152]{1,0:T(8,128)}) fusion(bf16[384,1152]{1,0:T(8,128)(2,1)S(1)} %copy-done.5, f32[384]{0:T(512)S(1)} %add_rsqrt_fusion, f32[384,1152]{1,0:T(8,128)} %convolution_add_fusion.4, bf16[384,1152]{1,0:T(8,128)(2,1)} %collective-permute-done.5, f32[]{:T(128)} %bitcast.39, f32[]{:T(128)} %bitcast.27), kind=kOutput, calls=%fused_computation.11 | convolution fusion | flops 684048000 | bytes 5311496 | tf_op jit(solution)/shard_map/dot_general | solution.py:201
  154.6 3.1 %fusion.5 = f32[384,1152]{1,0:T(8,128)} fusion(f32[384,1152]{1,0:T(8,128)} %get-tuple-element.14, bf16[384,1152]{1,0:T(8,128)(2,1)S(1)} %copy-done.5, f32[384]{0:T(512)S(1)} %get-tuple-element.13, f32[384]{0:T(512)S(1)} %add_rsqrt_fusion), kind=kLoop, calls=%fused_computation.13 | loop fusion | flops 2211840 | bytes 4426752 | tf_op jit(solution)/shard_map/mul | solution.py:227
  157.6 0.6 add_multiply_fusion
  (25 shorter events, 0.1 us)
Async XLA Ops:
  0.6 3.5 %copy-start = (bf16[1152,1152]{1,0:T(8,128)(2,1)S(1)}, bf16[1152,1152]{1,0:T(8,128)(2,1)}, u32[]{:S(2)}) copy-start(bf16[1152,1152]{1,0:T(8,128)(2,1)} %param.7) | copy-start | bytes 7962628
  0.6 3.5 %copy-start.1 = (bf16[384,1152]{1,0:T(8,128)(2,1)S(1)}, bf16[384,1152]{1,0:T(8,128)(2,1)}, u32[]{:S(2)}) copy-start(bf16[384,1152]{1,0:T(8,128)(2,1)} %a_ref.1) | copy-start | bytes 2654212
  3.6 17.4 %collective-permute-start = (bf16[384,1152]{1,0:T(8,128)(2,1)S(1)}, bf16[384,1152]{1,0:T(8,128)(2,1)}, u32[]{:S(2)}, u32[]{:S(2)}) collective-permute-start(bf16[384,1152]{1,0:T(8,128)(2,1)S(1)} %fusion.2), channel_id=1, source_target_pairs={{0,1},{1,2},{2,3},{3,4},{4,5},{5,6},{6,7},{7,8},{8,9},{9,10},{10,1... | collective-permute-start | bytes 2654216 | tf_op jit(solution)/shard_map/ppermute | solution.py:22
  5.7 8.6 %copy-start.2 = (f32[384,1152]{1,0:T(8,128)}, f32[384,1152]{1,0:T(8,128)S(1)}, u32[]{:S(2)}) copy-start(f32[384,1152]{1,0:T(8,128)S(1)} %get-tuple-element.4) | copy-start | bytes 5308420
  5.7 7.5 %copy-start.4 = (bf16[384,1152]{1,0:T(8,128)(2,1)S(1)}, bf16[384,1152]{1,0:T(8,128)(2,1)}, u32[]{:S(2)}) copy-start(bf16[384,1152]{1,0:T(8,128)(2,1)} %param.6) | copy-start | bytes 2654212
  5.9 22.3 %copy-start.8 = (bf16[384,1152]{1,0:T(8,128)(2,1)}, bf16[384,1152]{1,0:T(8,128)(2,1)S(1)}, u32[]{:S(2)}) copy-start(bf16[384,1152]{1,0:T(8,128)(2,1)S(1)} %multiply_convert_fusion.1) | copy-start | bytes 2654212
  5.9 20.3 %collective-permute-start.3 = (bf16[384,1152]{1,0:T(8,128)(2,1)S(1)}, bf16[384,1152]{1,0:T(8,128)(2,1)}, u32[]{:S(2)}, u32[]{:S(2)}) collective-permute-start(bf16[384,1152]{1,0:T(8,128)(2,1)S(1)} %multiply_convert_fusion.1), channel_id=1, source_target_pairs={{0,31},{1,0},{2,1},{3,2},{4,3},{5,4},{6,5},{7,6},{8,7},{9,8},{10,9... | collective-permute-start | bytes 2654216 | tf_op jit(solution)/shard_map/ppermute | solution.py:22
  21.0 17.3 %collective-permute-start.1 = (bf16[384,1152]{1,0:T(8,128)(2,1)}, bf16[384,1152]{1,0:T(8,128)(2,1)}, u32[]{:S(2)}, u32[]{:S(2)}) collective-permute-start(bf16[384,1152]{1,0:T(8,128)(2,1)} %collective-permute-done), channel_id=1, source_target_pairs={{0,1},{1,2},{2,3},{3,4},{4,5},{5,6},{6,7},{7,8},{8,9},{9,10},{10,1... | collective-permute-start | bytes 2654216 | tf_op jit(solution)/shard_map/ppermute | solution.py:22
  26.2 21.5 %collective-permute-start.4 = (bf16[384,1152]{1,0:T(8,128)(2,1)}, bf16[384,1152]{1,0:T(8,128)(2,1)}, u32[]{:S(2)}, u32[]{:S(2)}) collective-permute-start(bf16[384,1152]{1,0:T(8,128)(2,1)} %collective-permute-done.3), channel_id=1, source_target_pairs={{0,31},{1,0},{2,1},{3,2},{4,3},{5,4},{6,5},{7,6},{8,7},{9,8},{10,9... | collective-permute-start | bytes 2654216 | tf_op jit(solution)/shard_map/ppermute | solution.py:22
  38.3 24.2 %collective-permute-start.2 = (bf16[384,1152]{1,0:T(8,128)(2,1)}, bf16[384,1152]{1,0:T(8,128)(2,1)}, u32[]{:S(2)}, u32[]{:S(2)}) collective-permute-start(bf16[384,1152]{1,0:T(8,128)(2,1)} %collective-permute-done.1), channel_id=1, source_target_pairs={{0,1},{1,2},{2,3},{3,4},{4,5},{5,6},{6,7},{7,8},{8,9},{9,10},{10,1... | collective-permute-start | bytes 2654216 | tf_op jit(solution)/shard_map/ppermute | solution.py:22
  47.7 102.3 %collective-permute-start.5 = (bf16[384,1152]{1,0:T(8,128)(2,1)}, bf16[384,1152]{1,0:T(8,128)(2,1)}, u32[]{:S(2)}, u32[]{:S(2)}) collective-permute-start(bf16[384,1152]{1,0:T(8,128)(2,1)} %collective-permute-done.4), channel_id=1, source_target_pairs={{0,31},{1,0},{2,1},{3,2},{4,3},{5,4},{6,5},{7,6},{8,7},{9,8},{10,9... | collective-permute-start | bytes 2654216 | tf_op jit(solution)/shard_map/ppermute | solution.py:22
  51.4 3.1 %copy-start.7 = (f32[384,1152]{1,0:T(8,128)S(1)}, f32[384,1152]{1,0:T(8,128)}, u32[]{:S(2)}) copy-start(f32[384,1152]{1,0:T(8,128)} %convolution_add_fusion.2) | copy-start | bytes 5308420
  62.5 3.1 %copy-start.3 = (f32[384,1152]{1,0:T(8,128)S(1)}, f32[384,1152]{1,0:T(8,128)}, u32[]{:S(2)}) copy-start(f32[384,1152]{1,0:T(8,128)} %copy-done.2) | copy-start | bytes 5308420
  62.5 3.1 %copy-start.6 = (f32[384,1152]{1,0:T(8,128)S(1)}, f32[384,1152]{1,0:T(8,128)}, u32[]{:S(2)}) copy-start(f32[384,1152]{1,0:T(8,128)} %convolution_add_fusion.1) | copy-start | bytes 5308420
  147.2 2.7 %copy-start.5 = (bf16[384,1152]{1,0:T(8,128)(2,1)S(1)}, bf16[384,1152]{1,0:T(8,128)(2,1)}, u32[]{:S(2)}) copy-start(bf16[384,1152]{1,0:T(8,128)(2,1)} %param.6) | copy-start | bytes 2654212
  154.6 3.1 %copy-start.9 = (f32[384]{0:T(512)S(1)}, f32[384]{0:T(512)}, u32[]{:S(2)}) copy-start(f32[384]{0:T(512)} %get-tuple-element.7) | copy-start | bytes 4612
  154.6 3.1 %copy-start.10 = (f32[384]{0:T(512)S(1)}, f32[384]{0:T(512)}, u32[]{:S(2)}) copy-start(f32[384]{0:T(512)} %get-tuple-element.5) | copy-start | bytes 4612

commit v2 on v1

v2 whole, which is shorter than its diff:
```python
import functools

import jax
import jax.numpy as jnp
from jax import lax
from jax.experimental import pallas as pl
from jax.experimental.pallas import tpu as pltpu
from jax.sharding import PartitionSpec as P

STEPS = 4
PARTS = 3
TILE = 8
LANES = 128


epsilon = 1e-06


def bit_orders(count):
    levels = count.bit_length() - 1
    middle = list(range(1, levels - 1))
    orders = []
    for part in range(PARTS):
        turn = part % max(len(middle), 1)
        orders.append([0] + middle[turn:] + middle[:turn] + [levels - 1])
    return orders


def bit_of(me, bit):
    return lax.rem(lax.div(me, 1 << bit), 2)


def partner_of(me, bit):
    return me + (1 - 2 * bit_of(me, bit)) * (1 << bit)


def kernel(
    count, chunk, scale_ref, bias_ref, a_ref, t_ref, w_ref,
    loss_ref, tg_ref, out_ref,
    txt_bf, img_bf, img_unit, inv_t, inv_i, img_grad, unit_grad, g_ref, txt_in, img_in,
    total, landed,
    txt_send, txt_recv, img_send, img_recv, send_sem, recv_sem, back_send, back_recv,
):
    me = lax.axis_index("dp")
    orders = bit_orders(count)
    levels = count.bit_length() - 1
    local_rows = a_ref.shape[0]
    width = a_ref.shape[1] // PARTS
    blocks = g_ref.shape[1] // LANES
    rows = width // TILE
    used = blocks * rows
    full = count * chunk
    temper = scale_ref[0]
    offset_bias = bias_ref[0]

    odd = lax.rem(me, 2)
    mate = me + 1 - 2 * odd
    ahead = lax.rem(me + 2, count)
    behind = lax.rem(me + count - 2, count)
    far = lax.rem(me + count - 3 + 6 * odd, count)
    text_third = mate * (1 - odd) + far * odd
    image_third = mate * odd + far * (1 - odd)

    barrier = pltpu.get_barrier_semaphore()
    peers = [partner_of(me, bit) for bit in range(levels)] + [ahead, behind, far]
    for peer in peers:
        pl.semaphore_signal(
            barrier, inc=1, device_id=(peer,), device_id_type=pl.DeviceIdType.MESH
        )

    def remote(source, target, send, recv, device):
        return pltpu.make_async_remote_copy(
            src_ref=source, dst_ref=target, send_sem=send, recv_sem=recv,
            device_id=(device,), device_id_type=pl.DeviceIdType.MESH,
        )

    text_float = t_ref[...].astype(jnp.float32)
    inverse = lax.rsqrt(jnp.sum(text_float * text_float, axis=1, keepdims=True) + epsilon)
    inv_t[...] = inverse
    txt_bf[...] = (text_float * inverse).astype(jnp.bfloat16)
    pl.semaphore_wait(barrier, len(peers))

    text_copies = [
        remote(txt_bf, txt_in.at[0], txt_send.at[0], txt_recv.at[0], ahead),
        remote(txt_bf, txt_in.at[1], txt_send.at[1], txt_recv.at[1], text_third),
        remote(txt_in.at[0], txt_in.at[2], txt_send.at[2], txt_recv.at[2], mate),
    ]
    image_copies = [
        remote(img_bf, img_in.at[0], img_send.at[0], img_recv.at[0], behind),
        remote(img_bf, img_in.at[1], img_send.at[1], img_recv.at[1], image_third),
        remote(img_in.at[0], img_in.at[2], img_send.at[2], img_recv.at[2], mate),
    ]
    text_copies[0].start()
    text_copies[1].start()

    projected = jnp.dot(a_ref[...], w_ref[...], preferred_element_type=jnp.float32)
    inverse = lax.rsqrt(jnp.sum(projected * projected, axis=1, keepdims=True) + epsilon)
    inv_i[...] = inverse
    img_unit[...] = projected * inverse
    img_bf[...] = img_unit[...].astype(jnp.bfloat16)

    def scored(left, right):
        scores = lax.dot_general(
            left, right, (((1,), (1,)), ((), ())), preferred_element_type=jnp.float32
        )
        return temper * scores + offset_bias

    def sigmoid_of(value):
        small = jnp.exp(-jnp.abs(value))
        share = 1.0 / (1.0 + small)
        return small, jnp.where(value >= 0.0, share, small * share)

    def image_side(texts, own):
        logits = scored(img_bf[...], texts[...])
        if own:
            where = lax.broadcasted_iota(jnp.int32, logits.shape, 0)
            same = where == lax.broadcasted_iota(jnp.int32, logits.shape, 1)
            target = jnp.where(same, 1.0, -1.0)
            opposed = -target * logits
            small, slope = sigmoid_of(opposed)
            coefficient = (-target * temper * slope).astype(jnp.bfloat16)
        else:
            opposed = logits
            small, slope = sigmoid_of(opposed)
            coefficient = (temper * slope).astype(jnp.bfloat16)
        part = jnp.sum(jnp.maximum(opposed, 0.0) + jnp.log1p(small), axis=1, keepdims=True)
        grad = jnp.dot(coefficient, texts[...], preferred_element_type=jnp.float32)
        if own:
            loss_ref[...] = part
            img_grad[...] = grad
            unit_grad[...] = lax.dot_general(
                coefficient, img_bf[...], (((0,), (0,)), ((), ())),
                preferred_element_type=jnp.float32,
            )
        else:
            loss_ref[...] += part
            img_grad[...] += grad

    def text_side(images):
        slope = sigmoid_of(scored(txt_bf[...], images[...]))[1]
        coefficient = (temper * slope).astype(jnp.bfloat16)
        unit_grad[...] += jnp.dot(coefficient, images[...], preferred_element_type=jnp.float32)

    image_side(txt_bf, True)
    text_copies[0].wait_recv()
    text_copies[2].start()
    image_side(txt_in.at[0], False)
    text_copies[1].wait_recv()
    image_copies[0].start()
    image_copies[1].start()
    image_side(txt_in.at[1], False)
    text_copies[2].wait_recv()
    image_side(txt_in.at[2], False)
    loss_ref[...] = loss_ref[...] / (STEPS * local_rows)
    inner = jnp.sum(img_unit[...] * img_grad[...], axis=1, keepdims=True)
    g_ref[...] = ((img_grad[...] - img_unit[...] * inner) * inv_i[...]).astype(jnp.bfloat16)

    def first_image():
        image_copies[0].wait_recv()
        image_copies[2].start()
        text_side(img_in.at[0])

    def second_image():
        image_copies[1].wait_recv()
        text_side(img_in.at[1])

    def third_image():
        image_copies[2].wait_recv()
        text_side(img_in.at[2])

    def finish_text():
        unit = t_ref[...].astype(jnp.float32) * inv_t[...]
        inner = jnp.sum(unit * unit_grad[...], axis=1, keepdims=True)
        tg_ref[...] = (unit_grad[...] - unit * inner) * inv_t[...]

    def copy_at(part, step, start):
        half = full >> (step + 1)
        bit = orders[part][step]
        base = full - (full >> step)
        return remote(
            total.at[part, pl.ds(start + (1 - bit_of(me, bit)) * half, half)],
            landed.at[part, pl.ds(base, half)],
            send_sem.at[part, step], recv_sem.at[part, step], partner_of(me, bit),
        )

    def add(part, where, source, length):
        size = chunk
        while size < 16 and length % (2 * size) == 0:
            size *= 2

        def body(i, carry):
            total[part, pl.ds(where + i * size, size)] += landed[part, pl.ds(source + i * size, size)]
            return carry

        lax.fori_loop(0, length // size, body, 0)

    copies = {}
    starts = [0] * PARTS
    for part in range(PARTS):
        product = lax.dot_general(
            a_ref[:, part * width:(part + 1) * width], g_ref[...],
            (((0,), (0,)), ((), ())), preferred_element_type=jnp.float32,
        )
        for block in range(blocks):
            total[part, pl.ds(block, rows, stride=blocks)] = product[
                :, block * LANES:(block + 1) * LANES
            ].reshape(rows, TILE, LANES)
        if full > used:
            total[part, used:] = jnp.zeros((full - used, TILE, LANES), jnp.float32)
        copies[part, 0] = copy_at(part, 0, 0)
        copies[part, 0].start()
    for step in range(levels):
        half = full >> (step + 1)
        base = full - (full >> step)
        for part in range(PARTS):
            copies[part, step].wait_recv()
            start = starts[part] + bit_of(me, orders[part][step]) * half
            starts[part] = start
            if step + 1 < levels:
                quarter = half // 2
                mine = bit_of(me, orders[part][step + 1])
                away, kept = (1 - mine) * quarter, mine * quarter
                add(part, start + away, base + away, quarter)
                copies[part, step + 1] = copy_at(part, step + 1, start)
                copies[part, step + 1].start()
                add(part, start + kept, base + kept, quarter)
            else:
                out_ref[part, pl.ds(start, half)] = (
                    total[part, pl.ds(start, half)] + landed[part, pl.ds(base, half)]
                ) * (1.0 / count)
        if step == 1:
            first_image()
    backs = {}
    for step in reversed(range(levels)):
        length = full >> (step + 1)
        for part in range(PARTS):
            if step + 1 < levels:
                backs[part, step + 1].wait_recv()
                bit = orders[part][step + 1]
                starts[part] = starts[part] - bit_of(me, bit) * (length // 2)
            where = out_ref.at[part, pl.ds(starts[part], length)]
            backs[part, step] = remote(
                where, where, back_send.at[part, step], back_recv.at[part, step],
                partner_of(me, orders[part][step]),
            )
            backs[part, step].start()
        if step == 2:
            second_image()
        if step == 1:
            third_image()
        if step == 0:
            finish_text()
    for part in range(PARTS):
        backs[part, 0].wait_recv()
    for copy in text_copies + image_copies + list(copies.values()) + list(backs.values()):
        copy.wait_send()


def shards(image_pooled, text_embed, head_weight, logit_scale, logit_bias):
    count = lax.axis_size("dp")
    levels = count.bit_length() - 1
    local_rows, depth = image_pooled.shape
    width = head_weight.shape[1]
    used = depth * width // (PARTS * TILE * LANES)
    chunk = -(-used // count)
    full = chunk * count
    vmem = pl.BlockSpec(memory_space=pltpu.VMEM)
    smem = pl.BlockSpec(memory_space=pltpu.SMEM)
    loss, text_grad, every = pl.pallas_call(
        functools.partial(kernel, count, chunk),
        out_shape=(
            jax.ShapeDtypeStruct((local_rows, 1), jnp.float32),
            jax.ShapeDtypeStruct((local_rows, width), jnp.float32),
            jax.ShapeDtypeStruct((PARTS, full, TILE, LANES), jnp.float32),
        ),
        in_specs=[smem, smem, vmem, vmem, vmem],
        out_specs=(vmem, vmem, vmem),
        scratch_shapes=[
            pltpu.VMEM((local_rows, width), jnp.bfloat16),
            pltpu.VMEM((local_rows, width), jnp.bfloat16),
            pltpu.VMEM((local_rows, width), jnp.float32),
            pltpu.VMEM((local_rows, 1), jnp.float32),
            pltpu.VMEM((local_rows, 1), jnp.float32),
            pltpu.VMEM((local_rows, width), jnp.float32),
            pltpu.VMEM((local_rows, width), jnp.float32),
            pltpu.VMEM((local_rows, width), jnp.bfloat16),
            pltpu.VMEM((STEPS - 1, local_rows, width), jnp.bfloat16),
            pltpu.VMEM((STEPS - 1, local_rows, width), jnp.bfloat16),
            pltpu.VMEM((PARTS, full, TILE, LANES), jnp.float32),
            pltpu.VMEM((PARTS, full, TILE, LANES), jnp.float32),
        ] + [pltpu.SemaphoreType.DMA((STEPS - 1,))] * 4
        + [pltpu.SemaphoreType.DMA((PARTS, levels))] * 4,
        compiler_params=pltpu.CompilerParams(
            collective_id=0, has_side_effects=True, vmem_limit_bytes=56 * 1024 * 1024
        ),
        name="window_and_head",
    )(logit_scale, logit_bias, image_pooled, text_embed, head_weight)
    head = every[:, :used].reshape(depth // TILE, width // LANES, TILE, LANES)
    head = head.transpose(0, 2, 1, 3).reshape(depth, width)
    return (loss.reshape(local_rows), text_grad, head)


def solution(mesh):
    in_specs = (P("dp", None), P("dp", None), P(), P(), P())
    out_specs = (P("dp"), P("dp", None), P())
    return jax.shard_map(shards, mesh=mesh, in_specs=in_specs, out_specs=out_specs, check_vma=False)
```

time: 159 us -> 146 us (0.918)
  Pallas kernels: 79 us -> 136 us
  matrix products: 36.4 us -> 0 us
  starting transfers between devices: 26.8 us -> 0 us
  other arithmetic: 7.1 us -> 1.65 us
  waiting for transfers between devices: 4.04 us -> 0 us
  local copies, waits for them, and re-layouts: 2.77 us -> 6.57 us
    pallas_call x1, Pallas kernels: 79 us -> 136 us  [shards(): pl.pallas_call(functools.partial(kernel, count, chunk), out_shape=(jax.Sh...]
    dot_general x13 -> x0, matrix products: 36.4 us -> none  [the longest x4 16.2 us: text_side(): lax.dot_general(coefficient, images, (((0,), (0,)), ((), ())), preferred_...]
    ppermute x6 -> x0, starting transfers between devices: 26.8 us -> none  [shifted(): return lax.ppermute(value, axis, pairs)]
    ppermute x6 -> x0, waiting for transfers between devices: 4.04 us -> none  [shifted(): return lax.ppermute(value, axis, pairs)]
    mul x1 -> x0, other arithmetic: 3.05 us -> none  [shards(): (unit_grad - txt_unit * jnp.sum(txt_unit * unit_grad, axis=1, keepdims=Tr...]
    slice x1, local copies, waits for them, and re-layouts: 2.72 us -> 5.36 us  [shards(): head = every[:, :used].reshape(depth // TILE, width // LANES, TILE, LANES)]
    convert_element_type x3 -> x0, other arithmetic: 1.88 us -> none  [the longest x1 1.38 us: shards(): txt_bf = txt_unit.astype(jnp.bfloat16)]
    pallas_call x0 -> x1, other arithmetic: none -> 1.65 us  [shards(): pl.pallas_call(functools.partial(kernel, count, chunk), out_shape=(jax.Sh...]
  transfers between devices with their start and end apart: 6 -> 0, of which waited for: 1 -> 0; matrix products, arithmetic and copies ran while one was open for 22% -> 0% of each run, Pallas kernels for 50% -> 0%
where the time goes in v2:
time: 146 us
  Pallas kernels  136 us (93%)
  local copies, waits for them, and re-layouts  6.57 us (4%)
  between operations  1.93 us (1%)
  other arithmetic  1.65 us (1%)
    pallas_call x1, Pallas kernels, shards(): pl.pallas_call(functools.partial(kernel, count, chunk), out_shape=(jax.Sh...  136 us
    slice x1, local copies, waits for them, and re-layouts, shards(): head = every[:, :used].reshape(depth // TILE, width // LANES, TILE, LANES)  5.36 us

profile of v2, /device:TPU:0, one launch (start us, length us, event | category | flops | bytes accessed | tf_op | source)
XLA Modules:
  0.0 145.8 jit_solution(2170317360658270817)
XLA Ops:
  1.9 135.6 %window_and_head.1 = (f32[384,1]{1,0:T(8,128)}, f32[384,1152]{1,0:T(8,128)}, f32[3,448,8,128]{3,2,1,0:T(8,128)}) custom-call(f32[1]{0:T(128)S(6)} %copy.9.scale_ref, f32[1]{0:T(128)S(6)} %copy.10.bias_ref, bf16[384,1152]{1,0:T(8,128)(2,1)} %a_ref.1, bf16[384,1152]{1,0:T(8,128)(2,1)} %t_ref.1, bf16[1152,1152]{1,0:T(8,128)(2,1)} %w_ref.1), custom_call_target="tpu_custom_call" | custom-call | tf_op jit(solution)/shard_map/window_and_head/pallas_call | solution.py:269
  137.6 1.7 %reduce = f32[384]{0:T(512)} reduce(f32[384,1]{1,0:T(8,128)} %get-tuple-element.6, f32[]{:T(128)} %constant), dimensions={1}, to_apply=%get-tuple-element.6.reduce_sub_computation | reduce | bytes 3076 | tf_op jit(solution)/shard_map/window_and_head/pallas_call | solution.py:269
  139.2 0.0 copy-start
  139.2 5.4 %slice.3 = f32[3,432,8,128]{3,2,1,0:T(8,128)} slice(f32[3,448,8,128]{3,2,1,0:T(8,128)} %get-tuple-element.8), slice={[0:3], [0:432], [0:8], [0:128]} | slice | bytes 10616832 | tf_op jit(solution)/shard_map/slice | solution.py:298
  144.6 0.0 copy-done
  144.6 1.2 copy.11
Async XLA Ops:
  139.2 5.4 %copy-start = (f32[384,1152]{1,0:T(8,128)S(1)}, f32[384,1152]{1,0:T(8,128)}, u32[]{:S(2)}) copy-start(f32[384,1152]{1,0:T(8,128)} %get-tuple-element.13) | copy-start | bytes 5308420

commit v3 on v2

--- a/solution.py
+++ b/solution.py
@@ -11,6 +11,7 @@
 PARTS = 3
 TILE = 8
 LANES = 128
+PIECES = 4
 
 
 epsilon = 1e-06
@@ -22,7 +23,7 @@
     orders = []
     for part in range(PARTS):
         turn = part % max(len(middle), 1)
-        orders.append([0] + middle[turn:] + middle[:turn] + [levels - 1])
+        orders.append(middle[turn:] + middle[:turn] + [levels - 1])
     return orders
 
 
@@ -38,18 +39,20 @@
     count, chunk, scale_ref, bias_ref, a_ref, t_ref, w_ref,
     loss_ref, tg_ref, out_ref,
     txt_bf, img_bf, img_unit, inv_t, inv_i, img_grad, unit_grad, g_ref, txt_in, img_in,
-    total, landed,
-    txt_send, txt_recv, img_send, img_recv, send_sem, recv_sem, back_send, back_recv,
+    turned, turned_in, g_in, total, landed,
+    txt_send, txt_recv, img_send, img_recv, pair_send, pair_recv,
+    send_sem, recv_sem, back_send, back_recv, over_send, over_recv,
 ):
     me = lax.axis_index("dp")
     orders = bit_orders(count)
-    levels = count.bit_length() - 1
+    bits = count.bit_length() - 1
+    levels = bits - 1
     local_rows = a_ref.shape[0]
     width = a_ref.shape[1] // PARTS
     blocks = g_ref.shape[1] // LANES
-    rows = width // TILE
+    rows = width // 2 // TILE
     used = blocks * rows
-    full = count * chunk
+    full = count // 2 * chunk
     temper = scale_ref[0]
     offset_bias = bias_ref[0]
 
@@ -62,7 +65,7 @@
     image_third = mate * odd + far * (1 - odd)
 
     barrier = pltpu.get_barrier_semaphore()
-    peers = [partner_of(me, bit) for bit in range(levels)] + [ahead, behind, far]
+    peers = [partner_of(me, bit) for bit in range(bits)] + [ahead, behind, far]
     for peer in peers:
         pl.semaphore_signal(
             barrier, inc=1, device_id=(peer,), device_id_type=pl.DeviceIdType.MESH
@@ -92,12 +95,22 @@
     ]
     text_copies[0].start()
     text_copies[1].start()
+    for part in range(PARTS):
+        columns = a_ref[:, part * width:(part + 1) * width]
+        turned[part] = columns.T.reshape(2, width // 2, local_rows)
+    pair_copies = [
+        remote(turned.at[:, 1 - odd], turned_in, pair_send.at[0], pair_recv.at[0], mate),
+        remote(g_ref, g_in, pair_send.at[1], pair_recv.at[1], mate),
+    ]
+    pair_copies[0].start()
 
     projected = jnp.dot(a_ref[...], w_ref[...], preferred_element_type=jnp.float32)
     inverse = lax.rsqrt(jnp.sum(projected * projected, axis=1, keepdims=True) + epsilon)
     inv_i[...] = inverse
     img_unit[...] = projected * inverse
     img_bf[...] = img_unit[...].astype(jnp.bfloat16)
+    image_copies[0].start()
+    image_copies[1].start()
 
     def scored(left, right):
         scores = lax.dot_general(
@@ -146,14 +159,13 @@
     text_copies[2].start()
     image_side(txt_in.at[0], False)
     text_copies[1].wait_recv()
-    image_copies[0].start()
-    image_copies[1].start()
     image_side(txt_in.at[1], False)
     text_copies[2].wait_recv()
     image_side(txt_in.at[2], False)
     loss_ref[...] = loss_ref[...] / (STEPS * local_rows)
     inner = jnp.sum(img_unit[...] * img_grad[...], axis=1, keepdims=True)
     g_ref[...] = ((img_grad[...] - img_unit[...] * inner) * inv_i[...]).astype(jnp.bfloat16)
+    pair_copies[1].start()
 
     def first_image():
         image_copies[0].wait_recv()
@@ -194,21 +206,26 @@
 
         lax.fori_loop(0, length // size, body, 0)
 
+    def spread(part, block, product):
+        return product[:, block * LANES:(block + 1) * LANES].reshape(rows, TILE, LANES)
+
+    for part in range(PARTS):
+        product = jnp.dot(turned[part, odd], g_ref[...], preferred_element_type=jnp.float32)
+        for block in range(blocks):
+            total[part, pl.ds(block, rows, stride=blocks)] = spread(part, block, product)
+        if full > used:
+            total[part, used:] = jnp.zeros((full - used, TILE, LANES), jnp.float32)
+    pair_copies[0].wait_recv()
+    pair_copies[1].wait_recv()
     copies = {}
     starts = [0] * PARTS
     for part in range(PARTS):
-        product = lax.dot_general(
-            a_ref[:, part * width:(part + 1) * width], g_ref[...],
-            (((0,), (0,)), ((), ())), preferred_element_type=jnp.float32,
-        )
+        product = jnp.dot(turned_in[part], g_in[...], preferred_element_type=jnp.float32)
         for block in range(blocks):
-            total[part, pl.ds(block, rows, stride=blocks)] = product[
-                :, block * LANES:(block + 1) * LANES
-            ].reshape(rows, TILE, LANES)
-        if full > used:
-            total[part, used:] = jnp.zeros((full - used, TILE, LANES), jnp.float32)
+            total[part, pl.ds(block, rows, stride=blocks)] += spread(part, block, product)
         copies[part, 0] = copy_at(part, 0, 0)
         copies[part, 0].start()
+    first_image()
     for step in range(levels):
         half = full >> (step + 1)
         base = full - (full >> step)
@@ -225,45 +242,66 @@
                 copies[part, step + 1].start()
                 add(part, start + kept, base + kept, quarter)
             else:
-                out_ref[part, pl.ds(start, half)] = (
+                out_ref[part, odd, pl.ds(start, half)] = (
                     total[part, pl.ds(start, half)] + landed[part, pl.ds(base, half)]
                 ) * (1.0 / count)
-        if step == 1:
-            first_image()
-    backs = {}
-    for step in reversed(range(levels)):
-        length = full >> (step + 1)
-        for part in range(PARTS):
-            if step + 1 < levels:
-                backs[part, step + 1].wait_recv()
-                bit = orders[part][step + 1]
-                starts[part] = starts[part] - bit_of(me, bit) * (length // 2)
-            where = out_ref.at[part, pl.ds(starts[part], length)]
-            backs[part, step] = remote(
-                where, where, back_send.at[part, step], back_recv.at[part, step],
-                partner_of(me, orders[part][step]),
-            )
-            backs[part, step].start()
-        if step == 2:
+        if step == 0:
             second_image()
         if step == 1:
             third_image()
+    backs = {}
+    overs = []
+
+    def send_over(part, slot, start, length):
+        where = out_ref.at[part, odd, pl.ds(start, length)]
+        copy = remote(where, where, over_send.at[part, slot], over_recv.at[part, slot], mate)
+        copy.start()
+        overs.append(copy)
+
+    for step in reversed(range(levels)):
+        length = full >> (step + 1)
+        pieces = PIECES if step == 0 and length % PIECES == 0 else 1
+        piece = length // pieces
+        for part in range(PARTS):
+            start = starts[part]
+            for i in range(pieces):
+                where = out_ref.at[part, odd, pl.ds(start + i * piece, piece)]
+                slot = i if step == 0 else step + PIECES - 1
+                backs[part, step, i] = remote(
+                    where, where, back_send.at[part, slot], back_recv.at[part, slot],
+                    partner_of(me, orders[part][step]),
+                )
+                backs[part, step, i].start()
+            if step + 1 == levels:
+                send_over(part, levels + PIECES - 1, start, length)
         if step == 0:
             finish_text()
-    for part in range(PARTS):
-        backs[part, 0].wait_recv()
-    for copy in text_copies + image_copies + list(copies.values()) + list(backs.values()):
+        for i in range(pieces):
+            for part in range(PARTS):
+                backs[part, step, i].wait_recv()
+                bit = bit_of(me, orders[part][step])
+                other = starts[part] + (1 - 2 * bit) * length
+                slot = i if step == 0 else step + PIECES - 1
+                send_over(part, slot, other + i * piece, piece)
+        for part in range(PARTS):
+            starts[part] = starts[part] - bit_of(me, orders[part][step]) * length
+    for copy in overs:
+        copy.wait_recv()
+    for copy in (
+        text_copies + image_copies + pair_copies
+        + list(copies.values()) + list(backs.values()) + overs
+    ):
         copy.wait_send()
 
 
 def shards(image_pooled, text_embed, head_weight, logit_scale, logit_bias):
     count = lax.axis_size("dp")
-    levels = count.bit_length() - 1
+    levels = count.bit_length() - 2
     local_rows, depth = image_pooled.shape
     width = head_weight.shape[1]
-    used = depth * width // (PARTS * TILE * LANES)
-    chunk = -(-used // count)
-    full = chunk * count
+    used = depth * width // (PARTS * 2 * TILE * LANES)
+    chunk = -(-used // (count // 2))
+    full = chunk * (count // 2)
     vmem = pl.BlockSpec(memory_space=pltpu.VMEM)
     smem = pl.BlockSpec(memory_space=pltpu.SMEM)
     loss, text_grad, every = pl.pallas_call(
@@ -271,7 +309,7 @@
         out_shape=(
             jax.ShapeDtypeStruct((local_rows, 1), jnp.float32),
             jax.ShapeDtypeStruct((local_rows, width), jnp.float32),
-            jax.ShapeDtypeStruct((PARTS, full, TILE, LANES), jnp.float32),
+            jax.ShapeDtypeStruct((PARTS, 2, full, TILE, LANES), jnp.float32),
         ),
         in_specs=[smem, smem, vmem, vmem, vmem],
         out_specs=(vmem, vmem, vmem),
@@ -286,16 +324,20 @@
             pltpu.VMEM((local_rows, width), jnp.bfloat16),
             pltpu.VMEM((STEPS - 1, local_rows, width), jnp.bfloat16),
             pltpu.VMEM((STEPS - 1, local_rows, width), jnp.bfloat16),
+            pltpu.VMEM((PARTS, 2, depth // PARTS // 2, local_rows), jnp.bfloat16),
+            pltpu.VMEM((PARTS, depth // PARTS // 2, local_rows), jnp.bfloat16),
+            pltpu.VMEM((local_rows, width), jnp.bfloat16),
             pltpu.VMEM((PARTS, full, TILE, LANES), jnp.float32),
             pltpu.VMEM((PARTS, full, TILE, LANES), jnp.float32),
         ] + [pltpu.SemaphoreType.DMA((STEPS - 1,))] * 4
-        + [pltpu.SemaphoreType.DMA((PARTS, levels))] * 4,
+        + [pltpu.SemaphoreType.DMA((2,))] * 2
+        + [pltpu.SemaphoreType.DMA((PARTS, levels + PIECES))] * 6,
         compiler_params=pltpu.CompilerParams(
-            collective_id=0, has_side_effects=True, vmem_limit_bytes=56 * 1024 * 1024
+            collective_id=0, has_side_effects=True, vmem_limit_bytes=44 * 1024 * 1024
         ),
         name="window_and_head",
     )(logit_scale, logit_bias, image_pooled, text_embed, head_weight)
-    head = every[:, :used].reshape(depth // TILE, width // LANES, TILE, LANES)
+    head = every[:, :, :used].reshape(depth // TILE, width // LANES, TILE, LANES)
     head = head.transpose(0, 2, 1, 3).reshape(depth, width)
     return (loss.reshape(local_rows), text_grad, head)
 

time: 146 us -> 138 us (0.945)
  Pallas kernels: 136 us -> 124 us
  local copies, waits for them, and re-layouts: 6.57 us -> 10.5 us
    pallas_call x1, Pallas kernels: 136 us -> 124 us  [shards(): pl.pallas_call(functools.partial(kernel, count, chunk), out_shape=(jax.Sh...]
    unnamed x3 -> x7, local copies, waits for them, and re-layouts: 1.21 us -> 5.28 us
where the time goes in v3:
time: 138 us
  Pallas kernels  124 us (90%)
  local copies, waits for them, and re-layouts  10.5 us (8%)
  between operations  1.94 us (1%)
    pallas_call x1, Pallas kernels, shards(): pl.pallas_call(functools.partial(kernel, count, chunk), out_shape=(jax.Sh...  124 us
    unnamed x7, local copies, waits for them, and re-layouts  5.28 us
    slice x1, local copies, waits for them, and re-layouts, shards(): every[:, :, :used].reshape(depth // TILE, width // LANES, TILE, LANES)  5.23 us

profile of v3, /device:TPU:0, one launch (start us, length us, event | category | flops | bytes accessed | tf_op | source)
XLA Modules:
  0.0 137.6 jit_solution(10038834758675227051)
XLA Ops:
  1.9 0.0 copy-start
  1.9 1.7 %copy-done = bf16[1152,1152]{1,0:T(8,128)(2,1)S(1)} copy-done((bf16[1152,1152]{1,0:T(8,128)(2,1)S(1)}, bf16[1152,1152]{1,0:T(8,128)(2,1)}, u32[]{:S(2)}) %copy-start) | copy-done | bytes 2654232
  3.7 0.0 copy-start.1
  3.7 1.2 copy-done.1
  4.8 0.0 copy-start.2
  4.8 1.2 copy-done.2
  6.0 124.4 %window_and_head.1 = (f32[384,1]{1,0:T(8,128)S(1)}, f32[384,1152]{1,0:T(8,128)S(1)}, f32[3,2,224,8,128]{4,3,2,1,0:T(8,128)}) custom-call(f32[1]{0:T(128)S(6)} %copy.9.scale_ref, f32[1]{0:T(128)S(6)} %copy.10.bias_ref, bf16[384,1152]{1,0:T(8,128)(2,1)S(1)} %copy-done.1, bf16[384,1152]{1,0:T(8,128)(2,1)S(1)} %copy-done.2, bf16[1152,1152]{1,0:T(8,128)(2,1)S(1)} %copy-done), custom_call_target="tpu_custom_call" | custom-call | tf_op jit(solution)/shard_map/window_and_head/pallas_call | solution.py:307
  130.4 0.7 reduce
  131.2 5.2 %slice.3 = f32[3,2,216,8,128]{4,3,2,1,0:T(8,128)} slice(f32[3,2,224,8,128]{4,3,2,1,0:T(8,128)} %get-tuple-element.8), slice={[0:3], [0:2], [0:216], [0:8], [0:128]} | slice | bytes 10616832 | tf_op jit(solution)/shard_map/slice | solution.py:340
  136.4 1.2 copy.11
Async XLA Ops:
  1.9 1.8 %copy-start = (bf16[1152,1152]{1,0:T(8,128)(2,1)S(1)}, bf16[1152,1152]{1,0:T(8,128)(2,1)}, u32[]{:S(2)}) copy-start(bf16[1152,1152]{1,0:T(8,128)(2,1)} %w_ref.1) | copy-start | bytes 7962628
  3.7 1.2 copy-start.1
  4.8 1.2 copy-start.2

commit v4 on v3

--- a/solution.py
+++ b/solution.py
@@ -8,10 +8,10 @@
 from jax.sharding import PartitionSpec as P
 
 STEPS = 4
-PARTS = 3
+PARTS = 6
 TILE = 8
 LANES = 128
-PIECES = 4
+PIECES = 2
 
 
 epsilon = 1e-06
@@ -36,13 +36,19 @@
 
 
 def kernel(
-    count, chunk, scale_ref, bias_ref, a_ref, t_ref, w_ref,
+    count, chunk, scale_ref, bias_ref, a_hbm, t_hbm, w_hbm,
     loss_ref, tg_ref, out_ref,
-    txt_bf, img_bf, img_unit, inv_t, inv_i, img_grad, unit_grad, g_ref, txt_in, img_in,
+    a_ref, t_ref, w_ref, load_sem, txt_bf, img_bf, img_unit, inv_t, inv_i, img_grad, unit_grad, g_ref, txt_in, img_in,
     turned, turned_in, g_in, total, landed,
     txt_send, txt_recv, img_send, img_recv, pair_send, pair_recv,
     send_sem, recv_sem, back_send, back_recv, over_send, over_recv,
 ):
+    loads = [
+        pltpu.make_async_copy(source, target, load_sem.at[i])
+        for i, (source, target) in enumerate(((t_hbm, t_ref), (a_hbm, a_ref), (w_hbm, w_ref)))
+    ]
+    for load in loads:
+        load.start()
     me = lax.axis_index("dp")
     orders = bit_orders(count)
     bits = count.bit_length() - 1
@@ -77,6 +83,7 @@
             device_id=(device,), device_id_type=pl.DeviceIdType.MESH,
         )
 
+    loads[0].wait()
     text_float = t_ref[...].astype(jnp.float32)
     inverse = lax.rsqrt(jnp.sum(text_float * text_float, axis=1, keepdims=True) + epsilon)
     inv_t[...] = inverse
@@ -95,15 +102,17 @@
     ]
     text_copies[0].start()
     text_copies[1].start()
-    for part in range(PARTS):
-        columns = a_ref[:, part * width:(part + 1) * width]
-        turned[part] = columns.T.reshape(2, width // 2, local_rows)
+    loads[1].wait()
+    for part in range(0, PARTS, 2):
+        columns = a_ref[:, part * width:(part + 2) * width]
+        turned[part:part + 2] = columns.T.reshape(2, 2, width // 2, local_rows)
     pair_copies = [
         remote(turned.at[:, 1 - odd], turned_in, pair_send.at[0], pair_recv.at[0], mate),
         remote(g_ref, g_in, pair_send.at[1], pair_recv.at[1], mate),
     ]
     pair_copies[0].start()
 
+    loads[2].wait()
     projected = jnp.dot(a_ref[...], w_ref[...], preferred_element_type=jnp.float32)
     inverse = lax.rsqrt(jnp.sum(projected * projected, axis=1, keepdims=True) + epsilon)
     inv_i[...] = inverse
@@ -303,6 +312,7 @@
     chunk = -(-used // (count // 2))
     full = chunk * (count // 2)
     vmem = pl.BlockSpec(memory_space=pltpu.VMEM)
+    hbm = pl.BlockSpec(memory_space=pltpu.HBM)
     smem = pl.BlockSpec(memory_space=pltpu.SMEM)
     loss, text_grad, every = pl.pallas_call(
         functools.partial(kernel, count, chunk),
@@ -311,9 +321,13 @@
             jax.ShapeDtypeStruct((local_rows, width), jnp.float32),
             jax.ShapeDtypeStruct((PARTS, 2, full, TILE, LANES), jnp.float32),
         ),
-        in_specs=[smem, smem, vmem, vmem, vmem],
+        in_specs=[smem, smem, hbm, hbm, hbm],
         out_specs=(vmem, vmem, vmem),
         scratch_shapes=[
+            pltpu.VMEM((local_rows, depth), jnp.bfloat16),
+            pltpu.VMEM((local_rows, width), jnp.bfloat16),
+            pltpu.VMEM((depth, width), jnp.bfloat16),
+            pltpu.SemaphoreType.DMA((3,)),
             pltpu.VMEM((local_rows, width), jnp.bfloat16),
             pltpu.VMEM((local_rows, width), jnp.bfloat16),
             pltpu.VMEM((local_rows, width), jnp.float32),
@@ -333,7 +347,7 @@
         + [pltpu.SemaphoreType.DMA((2,))] * 2
         + [pltpu.SemaphoreType.DMA((PARTS, levels + PIECES))] * 6,
         compiler_params=pltpu.CompilerParams(
-            collective_id=0, has_side_effects=True, vmem_limit_bytes=44 * 1024 * 1024
+            collective_id=0, has_side_effects=True, vmem_limit_bytes=56 * 1024 * 1024
         ),
         name="window_and_head",
     )(logit_scale, logit_bias, image_pooled, text_embed, head_weight)

time: 138 us -> 133 us (0.964)
  local copies, waits for them, and re-layouts: 10.5 us -> 6.57 us
    unnamed x7 -> x3, local copies, waits for them, and re-layouts: 5.28 us -> 1.21 us
    pallas_call x1, Pallas kernels: 124 us -> 123 us  [shards(): pl.pallas_call(functools.partial(kernel, count, chunk), out_shape=(jax.Sh...]
where the time goes in v4:
time: 133 us
  Pallas kernels  123 us (92%)
  local copies, waits for them, and re-layouts  6.57 us (5%)
  between operations  1.93 us (1%)
  other arithmetic  1.65 us (1%)
    pallas_call x1, Pallas kernels, shards(): pl.pallas_call(functools.partial(kernel, count, chunk), out_shape=(jax.Sh...  123 us
    slice x1, local copies, waits for them, and re-layouts, shards(): every[:, :, :used].reshape(depth // TILE, width // LANES, TILE, LANES)  5.36 us

profile of v4, /device:TPU:0, one launch (start us, length us, event | category | flops | bytes accessed | tf_op | source)
XLA Modules:
  0.0 133.0 jit_solution(14050199567917307276)
XLA Ops:
  1.9 122.9 %window_and_head.1 = (f32[384,1]{1,0:T(8,128)}, f32[384,1152]{1,0:T(8,128)}, f32[6,2,112,8,128]{4,3,2,1,0:T(8,128)}) custom-call(f32[1]{0:T(128)S(6)} %copy.9.scale_ref, f32[1]{0:T(128)S(6)} %copy.10.bias_ref, bf16[384,1152]{1,0:T(8,128)(2,1)} %a_hbm.1, bf16[384,1152]{1,0:T(8,128)(2,1)} %t_hbm.1, bf16[1152,1152]{1,0:T(8,128)(2,1)} %w_hbm.1), custom_call_target="tpu_custom_call" | custom-call | tf_op jit(solution)/shard_map/window_and_head/pallas_call | solution.py:317
  124.8 1.7 %reduce = f32[384]{0:T(512)} reduce(f32[384,1]{1,0:T(8,128)} %get-tuple-element.6, f32[]{:T(128)} %constant), dimensions={1}, to_apply=%get-tuple-element.6.reduce_sub_computation | reduce | bytes 3076 | tf_op jit(solution)/shard_map/window_and_head/pallas_call | solution.py:317
  126.4 0.0 copy-start
  126.4 5.4 %slice.3 = f32[6,2,108,8,128]{4,3,2,1,0:T(8,128)} slice(f32[6,2,112,8,128]{4,3,2,1,0:T(8,128)} %get-tuple-element.8), slice={[0:6], [0:2], [0:108], [0:8], [0:128]} | slice | bytes 10616832 | tf_op jit(solution)/shard_map/slice | solution.py:354
  131.8 0.0 copy-done
  131.8 1.2 copy.11
Async XLA Ops:
  126.4 5.4 %copy-start = (f32[384,1152]{1,0:T(8,128)S(1)}, f32[384,1152]{1,0:T(8,128)}, u32[]{:S(2)}) copy-start(f32[384,1152]{1,0:T(8,128)} %get-tuple-element.13) | copy-start | bytes 5308420
